TPU v7x, 32 devices: a whole 2x2x4 slice. The times are simulated.
32 devices in a mesh: groups: 2 (over y), date: 4 (over z), pix: 2 (over x), chan: 2 (over core).
Axes of the slice: x: 2, y: 2, z: 4, core: 2. Of those that a mesh axis runs over, the one named last changes fastest.
Arguments:
- frames: bfloat16 [128, 4, 64, 128], P(('groups', 'date'), 'pix'), parts along dimension 0, may hold values from -6 to 6
- spatial_weight: bfloat16 [3, 3, 64, 64], P(None, None, None, 'chan'), may hold values from -0.25 to 0.25
- spatial_bias: float32 [64], P('chan'), may hold values from -3 to 3
- temporal_weight: bfloat16 [64, 64, 16], P('date', 'chan'), may hold values from -0.1875 to 0.1875
- temporal_bias: float32 [16], replicated, may hold values from -4 to 4
- head_weight: float32 [16], replicated, may hold values from -3 to 3
- labels: int32 [8, 128], P(('groups', 'pix'), ('date', 'chan')), parts along dimension 0, may hold values 0 or 1
Outputs:
- logits: float32 [8, 128], P(('groups', 'pix'), ('date', 'chan')), parts along dimension 0
- grad_spatial: float32 [6, 3, 64, 64], P('groups', None, None, 'chan'), parts along dimension 0
- grad_temporal: float32 [64, 64, 32], P('date', 'chan', 'groups'), parts along dimension 2
There are 2 independent parts, one for each index of `groups`. A program takes and returns all parts, laid end to end along the dimension named above; an argument that names none is the same for every part. Nothing has to cross between parts.
All inputs are finite; a program needn't handle non-finite values. No bound on the sum of `labels` on one device may be relied on, other than what follows from the above.
Results may differ from a plain program's by a relative error of at most 0.024.
Values may be sent and summed in bfloat16 or wider, within the bound.
A program may use at most 64 MiB of HBM per device.

v0:
```python
import jax
import jax.numpy as jnp
from jax import lax
from jax.sharding import PartitionSpec as P


def with_halo(block, sides, width):
    for axis, dim in sides:
        count = lax.axis_size(axis)
        forward = [(i, i + 1) for i in range(count - 1)]
        backward = [(target, source) for source, target in forward]
        low = lax.ppermute(
            lax.slice_in_dim(block, block.shape[dim] - width, None, axis=dim), axis, forward
        )
        high = lax.ppermute(lax.slice_in_dim(block, 0, width, axis=dim), axis, backward)
        block = jnp.concatenate([low, block, high], axis=dim)
    return block


def shards(
    frames, spatial_weight, spatial_bias, temporal_weight, temporal_bias, head_weight, labels
):
    dates_here, rows, channels, columns = frames.shape
    padded = with_halo(frames, (("pix", 1),), 1)
    padded = jnp.pad(padded, ((0, 0), (0, 0), (0, 0), (1, 1)))
    preact = spatial_bias[None, None, :, None]
    for row_off in range(3):
        for col_off in range(3):
            window = padded[:, row_off : row_off + rows, :, col_off : col_off + columns]
            preact = preact + jnp.einsum(
                "ticj,co->tioj",
                window,
                spatial_weight[row_off, col_off],
                preferred_element_type=jnp.float32,
            )
    sigmoid_pre = jax.nn.sigmoid(preact)
    hidden = (preact * sigmoid_pre).astype(jnp.bfloat16)
    partial_feat = jnp.einsum(
        "tioj,tof->fij", hidden, temporal_weight, preferred_element_type=jnp.float32
    )
    feature = (
        lax.psum_scatter(partial_feat, ("date", "chan"), scatter_dimension=2, tiled=True)
        + temporal_bias[:, None, None]
    )
    sigmoid_feat = jax.nn.sigmoid(feature)
    logits = jnp.einsum("fij,f->ij", feature * sigmoid_feat, head_weight)
    dlogit = jax.nn.sigmoid(logits) - labels.astype(jnp.float32)
    feature_grad = (
        dlogit[None]
        * head_weight[:, None, None]
        * sigmoid_feat
        * (1.0 + feature * (1.0 - sigmoid_feat))
    ).astype(jnp.bfloat16)
    full_grad = lax.all_gather(feature_grad, ("date", "chan"), axis=2, tiled=True)
    temporal_part = jnp.einsum(
        "tioj,fij->tof", hidden, full_grad, preferred_element_type=jnp.float32
    )
    hidden_grad = jnp.einsum(
        "fij,tof->tioj", full_grad, temporal_weight, preferred_element_type=jnp.float32
    )
    preact_grad = (hidden_grad * sigmoid_pre * (1.0 + preact * (1.0 - sigmoid_pre))).astype(
        jnp.bfloat16
    )
    rows_out = []
    for row_off in range(3):
        cols_out = []
        for col_off in range(3):
            window = padded[:, row_off : row_off + rows, :, col_off : col_off + columns]
            cols_out.append(
                jnp.einsum("ticj,tioj->co", window, preact_grad, preferred_element_type=jnp.float32)
            )
        rows_out.append(jnp.stack(cols_out))
    spatial_part = jnp.stack(rows_out)
    grad_temporal = lax.psum(temporal_part, "pix")
    grad_spatial = lax.psum(spatial_part, ("date", "pix"))
    return (logits, grad_spatial, grad_temporal)


def solution(mesh):
    placed = (
        P(("groups", "date"), "pix", None, None),
        P(None, None, None, "chan"),
        P("chan"),
        P("date", "chan", None),
        P(),
        P(),
        P(("groups", "pix"), ("date", "chan")),
    )
    return jax.shard_map(
        shards,
        mesh=mesh,
        in_specs=placed,
        out_specs=(
            P(("groups", "pix"), ("date", "chan")),
            P("groups", None, None, "chan"),
            P("date", "chan", "groups"),
        ),
        check_vma=False,
    )
```

profile of v0, /device:TPU:0, one launch (start us, length us, event | category | flops | bytes accessed | tf_op | source)
XLA Modules:
  0.0 157.4 jit_solution(17748076628413484052)
XLA Ops:
  7.2 1.1 fusion.79
  8.4 4.9 %collective-permute-start = (bf16[16,1,64,128]{3,2,1,0:T(8,128)(2,1)S(1)}, bf16[16,1,64,128]{3,2,1,0:T(8,128)(2,1)S(1)}, u32[]{:S(2)}, u32[]{:S(2)}) collective-permute-start(bf16[16,1,64,128]{3,2,1,0:T(8,128)(2,1)S(1)} %get-tuple-element.11), channel_id=1, source_target_pairs={{0,2},{1,3},{4,6},{5,7},{8,10},{9,11},{12,14},{13,15},{16,18},{17,... | collective-permute-start | bytes 786440 | tf_op jit(solution)/shard_map/ppermute | solution.py:12
  13.3 1.4 collective-permute-start.1
  14.7 1.3 fusion.47
  16.0 2.8 %collective-permute-done = bf16[16,1,64,128]{3,2,1,0:T(8,128)(2,1)S(1)} collective-permute-done((bf16[16,1,64,128]{3,2,1,0:T(8,128)(2,1)S(1)}, bf16[16,1,64,128]{3,2,1,0:T(8,128)(2,1)S(1)}, u32[]{:S(2)}, u32[]{:S(2)}) %collective-permute-start) | collective-permute-done | bytes 262176 | tf_op jit(solution)/shard_map/ppermute | solution.py:12
  18.8 4.3 %collective-permute-done.1 = bf16[16,1,64,128]{3,2,1,0:T(8,128)(2,1)S(1)} collective-permute-done((bf16[16,1,64,128]{3,2,1,0:T(8,128)(2,1)S(1)}, bf16[16,1,64,128]{3,2,1,0:T(8,128)(2,1)S(1)}, u32[]{:S(2)}, u32[]{:S(2)}) %collective-permute-start.1) | collective-permute-done | bytes 262176 | tf_op jit(solution)/shard_map/ppermute | solution.py:15
  23.0 1.1 fusion.5
  24.2 0.4 fusion.40
  24.5 0.4 fusion.51
  26.2 1.2 multiply_convert_fusion
  27.6 0.8 copy.76
  28.4 1.7 %reshape.35 = f32[128,32]{1,0:T(8,128)} reshape(f32[128,2,16]{2,1,0:T(2,128)} %bitcast.179) | data formatting | bytes 32768
  30.2 2.2 %fusion.78 = (bf16[16,2,64,128]{3,2,1,0:T(8,128)(2,1)}, bf16[16,2,64,128]{3,2,1,0:T(8,128)(2,1)}, bf16[16,2,64,128]{3,2,1,0:T(8,128)(2,1)}, bf16[16,2,64,128]{3,...) fusion(bf16[16,4,64,130]{3,2,1,0:T(8,128)(2,1)S(1)} %fusion.5), kind=kLoop, calls=%fused_computation.104 | loop fusion | bytes 6291456 | tf_op jit(solution)/shard_map/slice | solution.py:29
  32.4 28.2 %reduce-scatter.4.cloned.1.call-done = f32[16,32]{1,0:T(8,128)} async-done(((f32[128,32]{1,0:T(8,128)}), f32[16,32]{1,0:T(8,128)}) %reduce-scatter.4.cloned.1.call-update) | async-done | bytes 2064
  60.6 0.8 reshape.36
  61.9 14.0 %all_gather.3 = bf16[16,2,128]{0,1,2:T(2,128)(2,1)S(1)} all-gather(bf16[16,2,16]{0,1,2:T(2,128)(2,1)S(1)} %copy.31), channel_id=1, replica_groups=mesh['groups'=2,'date'=4,'pix'=2,'chan'=2] {'date','chan'}, dimensions={2}, use_global_device_ids=true | all-gather | bytes 9216 | tf_op jit(solution)/shard_map/all_gather | solution.py:54
  75.9 1.4 fusion.16
  77.6 0.3 convolution_bitcast_fusion.4
  78.9 0.3 convolution_bitcast_fusion.6
  80.1 0.7 pad_maximum_fusion.2
  80.8 0.3 convolution_bitcast_fusion.1
  81.0 10.8 %psum.15 = f32[16,32,16]{1,2,0:T(8,128)} all-reduce(f32[16,32,16]{1,2,0:T(8,128)S(1)} %convolution_bitcast_fusion.1), channel_id=1, replica_groups=mesh['groups'=2,'date'=4,'pix'=2,'chan'=2] {'pix'}, use_global_device_ids=true, to_apply=%region_2.3 | all-reduce | flops 8192 | bytes 65536 | tf_op jit(solution)/shard_map/psum | solution.py:74
  91.8 57.2 %all-reduce.3.cloned.1.call-done = f32[3,3,64,32]{2,3,1,0:T(8,128)} async-done(((f32[3,3,64,32]{2,3,1,0:T(8,128)}), f32[3,3,64,32]{2,3,1,0:T(8,128)}) %all-reduce.3.cloned.1.call-update) | async-done | bytes 73744 | tf_op jit(solution)/shard_map/psum | solution.py:75
  149.0 1.6 %copy.115 = f32[3,3,64,32]{2,3,1,0:T(8,128)} copy(f32[3,3,64,32]{2,3,1,0:T(8,128)} %all-reduce.3.cloned.1.call-done) | data formatting | bytes 147456
  (58 shorter events, 4.3 us)
Async XLA Ops:
  7.2 20.3 %copy-start = (bf16[16,32,16]{1,2,0:T(8,128)(2,1)S(1)}, bf16[16,32,16]{1,2,0:T(8,128)(2,1)}, u32[]{:S(2)}) copy-start(bf16[16,32,16]{1,2,0:T(8,128)(2,1)} %param.10) | copy-start | bytes 49156
  7.2 15.9 %copy-start.1 = (bf16[16,2,64,128]{3,2,1,0:T(8,128)(2,1)S(1)}, bf16[16,2,64,128]{3,2,1,0:T(8,128)(2,1)}, u32[]{:S(2)}) copy-start(bf16[16,2,64,128]{3,2,1,0:T(8,128)(2,1)} %param.7) | copy-start | bytes 1572868
  7.2 53.4 %reduce-scatter.4.cloned.1.call-start = ((), (), s32[]{:S(2)}) async-start(), calls=%async_computation.2 | async-start | bytes 73728
  8.4 10.4 %collective-permute-start = (bf16[16,1,64,128]{3,2,1,0:T(8,128)(2,1)S(1)}, bf16[16,1,64,128]{3,2,1,0:T(8,128)(2,1)S(1)}, u32[]{:S(2)}, u32[]{:S(2)}) collective-permute-start(bf16[16,1,64,128]{3,2,1,0:T(8,128)(2,1)S(1)} %get-tuple-element.11), channel_id=1, source_target_pairs={{0,2},{1,3},{4,6},{5,7},{8,10},{9,11},{12,14},{13,15},{16,18},{17,... | collective-permute-start | bytes 786440 | tf_op jit(solution)/shard_map/ppermute | solution.py:12
  13.2 10.9 %copy-start.10 = (bf16[3,3,64,32]{2,3,1,0:T(8,128)(2,1)S(1)}, bf16[3,3,64,32]{2,3,1,0:T(8,128)(2,1)}, u32[]{:S(2)}) copy-start(bf16[3,3,64,32]{2,3,1,0:T(8,128)(2,1)} %param.8) | copy-start | bytes 110596
  13.3 9.8 %collective-permute-start.1 = (bf16[16,1,64,128]{3,2,1,0:T(8,128)(2,1)S(1)}, bf16[16,1,64,128]{3,2,1,0:T(8,128)(2,1)S(1)}, u32[]{:S(2)}, u32[]{:S(2)}) collective-permute-start(bf16[16,1,64,128]{3,2,1,0:T(8,128)(2,1)S(1)} %get-tuple-element.12), channel_id=1, source_target_pairs={{2,0},{3,1},{6,4},{7,5},{10,8},{11,9},{14,12},{15,13},{18,16},{19,... | collective-permute-start | bytes 786440 | tf_op jit(solution)/shard_map/ppermute | solution.py:15
  25.3 0.7 copy-start.15
  25.4 0.8 copy-start.2
  30.1 31.4 %copy-start.13 = (f32[16]{0:T(128)S(1)}, f32[16]{0:T(128)}, u32[]{:S(2)}) copy-start(f32[16]{0:T(128)} %param.11) | copy-start | bytes 196
  30.1 31.4 %copy-start.14 = (f32[16]{0:T(128)S(1)}, f32[16]{0:T(128)}, u32[]{:S(2)}) copy-start(f32[16]{0:T(128)} %param.12) | copy-start | bytes 196
  30.1 31.5 %copy-start.11 = (s32[2,16]{1,0:T(2,128)S(1)}, s32[2,16]{1,0:T(2,128)}, u32[]{:S(2)}) copy-start(s32[2,16]{1,0:T(2,128)} %param.13) | copy-start | bytes 388
  30.1 118.9 %all-reduce.3.cloned.1.call-start = ((), (), s32[]{:S(2)}) async-start(), calls=%async_computation.1 | async-start | bytes 294912 | tf_op jit(solution)/shard_map/psum | solution.py:75
  32.4 44.9 %copy-start.3 = (bf16[16,2,64,128]{3,2,1,0:T(8,128)(2,1)S(1)}, bf16[16,2,64,128]{3,2,1,0:T(8,128)(2,1)}, u32[]{:S(2)}) copy-start(bf16[16,2,64,128]{3,2,1,0:T(8,128)(2,1)} %copy-done.2) | copy-start | bytes 1572868
  61.6 16.2 %copy-start.12 = (f32[1,2,16]{2,0,1:T(1,128)}, f32[1,2,16]{2,0,1:T(1,128)S(1)}, u32[]{:S(2)}) copy-start(f32[1,2,16]{2,0,1:T(1,128)S(1)} %fusion.28) | copy-start | bytes 388
  77.3 1.0 copy-start.9
  77.3 1.3 copy-start.8
  77.6 1.3 copy-start.7
  77.9 1.3 copy-start.6
  78.1 1.3 copy-start.5
  78.6 1.2 copy-start.4
Sparse Core Ops, SparseCore 0:
  30.2 30.3 reduce-scatter.3
  80.9 68.0 all-reduce.2
where the time goes:
time: 158 us; the launch traced here: 157 us
  waiting for transfers between devices  92.5 us (59%)
  blocking collectives  24.7 us (16%)
  between operations  14.3 us (9%)
  local copies, waits for them, and re-layouts  8.89 us (6%)
  matrix products  8.7 us (6%)
  starting transfers between devices  6.36 us (4%)
  other arithmetic  1.98 us (1%)
    psum x1, waiting for transfers between devices, shards(): grad_spatial = lax.psum(spatial_part, ('date', 'pix'))  57.2 us
    unnamed x3, waiting for transfers between devices  28.2 us
    all_gather x1, blocking collectives, shards(): lax.all_gather(feature_grad, ('date', 'chan'), axis=2, tiled=True)  14 us
    psum x1, blocking collectives, shards(): grad_temporal = lax.psum(temporal_part, 'pix')  10.8 us
    unnamed x37, local copies, waits for them, and re-layouts  5.36 us
    ppermute x1, starting transfers between devices, with_halo(): lax.ppermute(lax.slice_in_dim(block, block.shape[dim] - width, None, axis...  4.86 us
    ppermute x1, waiting for transfers between devices, with_halo(): lax.ppermute(lax.slice_in_dim(block, 0, width, axis=dim), axis, backward)  4.27 us
    dot_general x9, matrix products, shards(): jnp.einsum('ticj,co->tioj', window, spatial_weight[row_off, col_off], pre...  4.27 us
  transfers between devices with their start and end apart: 4, of which 4 were waited for; matrix products, arithmetic and copies ran while one was open for 2% of the time, Pallas kernels for 0%

commit v1 on v0

--- a/solution.py
+++ b/solution.py
@@ -2,6 +2,19 @@
 import jax.numpy as jnp
 from jax import lax
 from jax.sharding import PartitionSpec as P
+
+
+def ring_gather(x, axis, dim):
+    ways = lax.axis_size(axis)
+    up = [(d, (d + 1) % ways) for d in range(ways)]
+    down = [(d, (d - 1) % ways) for d in range(ways)]
+    earlier, later = ([x], [x])
+    for _ in range(ways // 2):
+        earlier.append(lax.ppermute(earlier[-1], axis, up))
+    for _ in range((ways - 1) // 2):
+        later.append(lax.ppermute(later[-1], axis, down))
+    line = jnp.concatenate([*earlier[::-1], *later[1:]], axis=dim)
+    return jnp.roll(line, (lax.axis_index(axis) - ways // 2) * x.shape[dim], axis=dim)
 
 
 def with_halo(block, sides, width):
@@ -51,7 +64,7 @@
         * sigmoid_feat
         * (1.0 + feature * (1.0 - sigmoid_feat))
     ).astype(jnp.bfloat16)
-    full_grad = lax.all_gather(feature_grad, ("date", "chan"), axis=2, tiled=True)
+    full_grad = ring_gather(feature_grad, ("date", "chan"), 2)
     temporal_part = jnp.einsum(
         "tioj,fij->tof", hidden, full_grad, preferred_element_type=jnp.float32
     )

time: 158 us -> 164 us (1.038)
  blocking collectives: 24.7 us -> 10.2 us
  starting transfers between devices: 6.36 us -> 17 us
  waiting for transfers between devices: 92.5 us -> 102 us
    all_gather x1 -> x0, blocking collectives: 14 us -> none  [shards(): lax.all_gather(feature_grad, ('date', 'chan'), axis=2, tiled=True)]
    ppermute x0 -> x7, starting transfers between devices: none -> 10.7 us  [the longest x3 10.6 us: ring_gather(): later.append(lax.ppermute(later[-1], axis, down))]
    ppermute x0 -> x7, waiting for transfers between devices: none -> 6.62 us  [the longest x4 6.49 us: ring_gather(): earlier.append(lax.ppermute(earlier[-1], axis, up))]
    unnamed x3, waiting for transfers between devices: 28.2 us -> 30.5 us
  transfers between devices with their start and end apart: 4 -> 11, of which waited for: 4 -> 9; matrix products, arithmetic and copies ran while one was open for 2% -> 2% of each run, Pallas kernels for 0% -> 0%
where the time goes in v1:
time: 164 us; the launch traced here: 163 us
  waiting for transfers between devices  102 us (62%)
  starting transfers between devices  17 us (10%)
  between operations  14.3 us (9%)
  blocking collectives  10.2 us (6%)
  local copies, waits for them, and re-layouts  8.86 us (5%)
  matrix products  8.78 us (5%)
  other arithmetic  1.98 us (1%)
    psum x1, waiting for transfers between devices, shards(): grad_spatial = lax.psum(spatial_part, ('date', 'pix'))  58 us
    unnamed x3, waiting for transfers between devices  30.5 us
    ppermute x3, starting transfers between devices, ring_gather(): later.append(lax.ppermute(later[-1], axis, down))  10.6 us
    psum x1, blocking collectives, shards(): grad_temporal = lax.psum(temporal_part, 'pix')  10.2 us
    ppermute x4, waiting for transfers between devices, ring_gather(): earlier.append(lax.ppermute(earlier[-1], axis, up))  6.49 us
    unnamed x37, local copies, waits for them, and re-layouts  5.37 us
    ppermute x1, starting transfers between devices, with_halo(): lax.ppermute(lax.slice_in_dim(block, block.shape[dim] - width, None, axis...  4.86 us
    dot_general x9, matrix products, shards(): jnp.einsum('ticj,co->tioj', window, spatial_weight[row_off, col_off], pre...  4.29 us
  transfers between devices with their start and end apart: 11, of which 9 were waited for; matrix products, arithmetic and copies ran while one was open for 2% of the time, Pallas kernels for 0%

profile of v1, /device:TPU:0, one launch (start us, length us, event | category | flops | bytes accessed | tf_op | source)
XLA Modules:
  0.0 163.3 jit_solution(16796424278508233526)
XLA Ops:
  7.2 1.1 fusion.83
  8.4 4.9 %collective-permute-start = (bf16[16,1,64,128]{3,2,1,0:T(8,128)(2,1)S(1)}, bf16[16,1,64,128]{3,2,1,0:T(8,128)(2,1)S(1)}, u32[]{:S(2)}, u32[]{:S(2)}) collective-permute-start(bf16[16,1,64,128]{3,2,1,0:T(8,128)(2,1)S(1)} %get-tuple-element.11), channel_id=1, source_target_pairs={{0,2},{1,3},{4,6},{5,7},{8,10},{9,11},{12,14},{13,15},{16,18},{17,... | collective-permute-start | bytes 786440 | tf_op jit(solution)/shard_map/ppermute | solution.py:25
  13.3 1.4 collective-permute-start.1
  14.7 1.3 fusion.47
  16.0 2.8 %collective-permute-done = bf16[16,1,64,128]{3,2,1,0:T(8,128)(2,1)S(1)} collective-permute-done((bf16[16,1,64,128]{3,2,1,0:T(8,128)(2,1)S(1)}, bf16[16,1,64,128]{3,2,1,0:T(8,128)(2,1)S(1)}, u32[]{:S(2)}, u32[]{:S(2)}) %collective-permute-start) | collective-permute-done | bytes 262176 | tf_op jit(solution)/shard_map/ppermute | solution.py:25
  18.8 4.3 %collective-permute-done.1 = bf16[16,1,64,128]{3,2,1,0:T(8,128)(2,1)S(1)} collective-permute-done((bf16[16,1,64,128]{3,2,1,0:T(8,128)(2,1)S(1)}, bf16[16,1,64,128]{3,2,1,0:T(8,128)(2,1)S(1)}, u32[]{:S(2)}, u32[]{:S(2)}) %collective-permute-start.1) | collective-permute-done | bytes 262176 | tf_op jit(solution)/shard_map/ppermute | solution.py:28
  23.0 1.1 fusion.5
  26.3 1.2 multiply_convert_fusion
  27.7 0.8 copy.73
  28.4 1.7 %reshape.34 = f32[128,32]{1,0:T(8,128)} reshape(f32[128,2,16]{2,1,0:T(2,128)} %bitcast.178) | data formatting | bytes 32768
  30.2 30.5 %reduce-scatter.4.cloned.1.call-done = f32[16,32]{1,0:T(8,128)} async-done(((f32[128,32]{1,0:T(8,128)}), f32[16,32]{1,0:T(8,128)}) %reduce-scatter.4.cloned.1.call-update) | async-done | bytes 2064
  60.6 0.8 reshape.35
  61.9 3.5 %collective-permute-start.6 = (bf16[16,2,16]{2,0,1:T(8,128)(2,1)S(1)}, bf16[16,2,16]{2,0,1:T(8,128)(2,1)S(1)}, u32[]{:S(2)}, u32[]{:S(2)}) collective-permute-start(bf16[16,2,16]{2,0,1:T(8,128)(2,1)S(1)} %multiply_convert_fusion.1), channel_id=1, source_target_pairs={{0,13},{1,0},{4,1},{5,4},{8,5},{9,8},{12,9},{13,12},{2,15},{3,2},{... | collective-permute-start | bytes 3080 | tf_op jit(solution)/shard_map/ppermute | solution.py:15
  65.4 1.3 collective-permute-done.2
  66.8 3.6 %collective-permute-start.7 = (bf16[16,2,16]{2,0,1:T(8,128)(2,1)S(1)}, bf16[16,2,16]{2,0,1:T(8,128)(2,1)S(1)}, u32[]{:S(2)}, u32[]{:S(2)}) collective-permute-start(bf16[16,2,16]{2,0,1:T(8,128)(2,1)S(1)} %collective-permute-done.6), channel_id=1, source_target_pairs={{0,13},{1,0},{4,1},{5,4},{8,5},{9,8},{12,9},{13,12},{2,15},{3,2},{... | collective-permute-start | bytes 3080 | tf_op jit(solution)/shard_map/ppermute | solution.py:15
  70.3 1.3 collective-permute-done.3
  71.7 3.5 %collective-permute-start.8 = (bf16[16,2,16]{2,0,1:T(8,128)(2,1)S(1)}, bf16[16,2,16]{2,0,1:T(8,128)(2,1)S(1)}, u32[]{:S(2)}, u32[]{:S(2)}) collective-permute-start(bf16[16,2,16]{2,0,1:T(8,128)(2,1)S(1)} %collective-permute-done.7), channel_id=1, source_target_pairs={{0,13},{1,0},{4,1},{5,4},{8,5},{9,8},{12,9},{13,12},{2,15},{3,2},{... | collective-permute-start | bytes 3080 | tf_op jit(solution)/shard_map/ppermute | solution.py:15
  75.2 1.3 collective-permute-done.4
  76.5 2.2 %fusion.82 = (bf16[16,2,64,128]{3,2,1,0:T(8,128)(2,1)}, bf16[16,2,64,128]{3,2,1,0:T(8,128)(2,1)}, bf16[16,2,64,128]{3,2,1,0:T(8,128)(2,1)}, bf16[16,2,64,128]{3,...) fusion(bf16[16,4,64,130]{3,2,1,0:T(8,128)(2,1)S(1)} %fusion.5), kind=kLoop, calls=%fused_computation.108 | loop fusion | bytes 6291456 | tf_op jit(solution)/shard_map/slice | solution.py:42
  78.8 2.6 %collective-permute-done.5 = bf16[16,2,16]{2,0,1:T(8,128)(2,1)S(1)} collective-permute-done((bf16[16,2,16]{2,0,1:T(8,128)(2,1)S(1)}, bf16[16,2,16]{2,0,1:T(8,128)(2,1)S(1)}, u32[]{:S(2)}, u32[]{:S(2)}) %collective-permute-start.5) | collective-permute-done | bytes 1056 | tf_op jit(solution)/shard_map/ppermute | solution.py:13
  81.5 1.4 fusion.16
  86.7 10.2 %psum.15 = f32[16,32,16]{1,2,0:T(8,128)} all-reduce(f32[16,32,16]{1,2,0:T(8,128)S(1)} %convolution_bitcast_fusion.1), channel_id=1, replica_groups=mesh['groups'=2,'date'=4,'pix'=2,'chan'=2] {'pix'}, use_global_device_ids=true, to_apply=%region_2.3 | all-reduce | flops 8192 | bytes 65536 | tf_op jit(solution)/shard_map/psum | solution.py:87
  96.9 58.0 %all-reduce.3.cloned.1.call-done = f32[3,3,64,32]{2,3,1,0:T(8,128)} async-done(((f32[3,3,64,32]{2,3,1,0:T(8,128)}), f32[3,3,64,32]{2,3,1,0:T(8,128)}) %all-reduce.3.cloned.1.call-update) | async-done | bytes 73744 | tf_op jit(solution)/shard_map/psum | solution.py:88
  154.9 1.6 copy.112
  (70 shorter events, 6.8 us)
Async XLA Ops:
  7.2 20.3 %copy-start = (bf16[16,32,16]{1,2,0:T(8,128)(2,1)S(1)}, bf16[16,32,16]{1,2,0:T(8,128)(2,1)}, u32[]{:S(2)}) copy-start(bf16[16,32,16]{1,2,0:T(8,128)(2,1)} %param.10) | copy-start | bytes 49156
  7.2 15.9 %copy-start.1 = (bf16[16,2,64,128]{3,2,1,0:T(8,128)(2,1)S(1)}, bf16[16,2,64,128]{3,2,1,0:T(8,128)(2,1)}, u32[]{:S(2)}) copy-start(bf16[16,2,64,128]{3,2,1,0:T(8,128)(2,1)} %param.7) | copy-start | bytes 1572868
  7.2 53.4 %reduce-scatter.4.cloned.1.call-start = ((), (), s32[]{:S(2)}) async-start(), calls=%async_computation.2 | async-start | bytes 73728
  8.4 10.4 %collective-permute-start = (bf16[16,1,64,128]{3,2,1,0:T(8,128)(2,1)S(1)}, bf16[16,1,64,128]{3,2,1,0:T(8,128)(2,1)S(1)}, u32[]{:S(2)}, u32[]{:S(2)}) collective-permute-start(bf16[16,1,64,128]{3,2,1,0:T(8,128)(2,1)S(1)} %get-tuple-element.11), channel_id=1, source_target_pairs={{0,2},{1,3},{4,6},{5,7},{8,10},{9,11},{12,14},{13,15},{16,18},{17,... | collective-permute-start | bytes 786440 | tf_op jit(solution)/shard_map/ppermute | solution.py:25
  13.2 10.9 %copy-start.10 = (bf16[3,3,64,32]{2,3,1,0:T(8,128)(2,1)S(1)}, bf16[3,3,64,32]{2,3,1,0:T(8,128)(2,1)}, u32[]{:S(2)}) copy-start(bf16[3,3,64,32]{2,3,1,0:T(8,128)(2,1)} %param.8) | copy-start | bytes 110596
  13.3 9.8 %collective-permute-start.1 = (bf16[16,1,64,128]{3,2,1,0:T(8,128)(2,1)S(1)}, bf16[16,1,64,128]{3,2,1,0:T(8,128)(2,1)S(1)}, u32[]{:S(2)}, u32[]{:S(2)}) collective-permute-start(bf16[16,1,64,128]{3,2,1,0:T(8,128)(2,1)S(1)} %get-tuple-element.12), channel_id=1, source_target_pairs={{2,0},{3,1},{6,4},{7,5},{10,8},{11,9},{14,12},{15,13},{18,16},{19,... | collective-permute-start | bytes 786440 | tf_op jit(solution)/shard_map/ppermute | solution.py:28
  26.2 35.3 %copy-start.13 = (f32[16]{0:T(128)S(1)}, f32[16]{0:T(128)}, u32[]{:S(2)}) copy-start(f32[16]{0:T(128)} %param.11) | copy-start | bytes 196
  26.2 35.3 %copy-start.14 = (f32[16]{0:T(128)S(1)}, f32[16]{0:T(128)}, u32[]{:S(2)}) copy-start(f32[16]{0:T(128)} %param.12) | copy-start | bytes 196
  26.2 35.5 %copy-start.11 = (s32[2,16]{1,0:T(2,128)S(1)}, s32[2,16]{1,0:T(2,128)}, u32[]{:S(2)}) copy-start(s32[2,16]{1,0:T(2,128)} %param.13) | copy-start | bytes 388
  30.1 124.8 %all-reduce.3.cloned.1.call-start = ((), (), s32[]{:S(2)}) async-start(), calls=%async_computation.1 | async-start | bytes 294912 | tf_op jit(solution)/shard_map/psum | solution.py:88
  61.7 17.1 %copy-start.12 = (f32[1,2,16]{2,0,1:T(1,128)}, f32[1,2,16]{2,0,1:T(1,128)S(1)}, u32[]{:S(2)}) copy-start(f32[1,2,16]{2,0,1:T(1,128)S(1)} %fusion.28) | copy-start | bytes 388
  61.8 4.9 %collective-permute-start.2 = (bf16[16,2,16]{2,0,1:T(8,128)(2,1)S(1)}, bf16[16,2,16]{2,0,1:T(8,128)(2,1)S(1)}, u32[]{:S(2)}, u32[]{:S(2)}) collective-permute-start(bf16[16,2,16]{2,0,1:T(8,128)(2,1)S(1)} %multiply_convert_fusion.1), channel_id=1, source_target_pairs={{0,1},{1,4},{4,5},{5,8},{8,9},{9,12},{12,13},{13,0},{2,3},{3,6},{6... | collective-permute-start | bytes 3080 | tf_op jit(solution)/shard_map/ppermute | solution.py:13
  61.9 4.9 %collective-permute-start.6 = (bf16[16,2,16]{2,0,1:T(8,128)(2,1)S(1)}, bf16[16,2,16]{2,0,1:T(8,128)(2,1)S(1)}, u32[]{:S(2)}, u32[]{:S(2)}) collective-permute-start(bf16[16,2,16]{2,0,1:T(8,128)(2,1)S(1)} %multiply_convert_fusion.1), channel_id=1, source_target_pairs={{0,13},{1,0},{4,1},{5,4},{8,5},{9,8},{12,9},{13,12},{2,15},{3,2},{... | collective-permute-start | bytes 3080 | tf_op jit(solution)/shard_map/ppermute | solution.py:15
  66.7 4.9 %collective-permute-start.3 = (bf16[16,2,16]{2,0,1:T(8,128)(2,1)S(1)}, bf16[16,2,16]{2,0,1:T(8,128)(2,1)S(1)}, u32[]{:S(2)}, u32[]{:S(2)}) collective-permute-start(bf16[16,2,16]{2,0,1:T(8,128)(2,1)S(1)} %collective-permute-done.2), channel_id=1, source_target_pairs={{0,1},{1,4},{4,5},{5,8},{8,9},{9,12},{12,13},{13,0},{2,3},{3,6},{6... | collective-permute-start | bytes 3080 | tf_op jit(solution)/shard_map/ppermute | solution.py:13
  66.8 4.9 %collective-permute-start.7 = (bf16[16,2,16]{2,0,1:T(8,128)(2,1)S(1)}, bf16[16,2,16]{2,0,1:T(8,128)(2,1)S(1)}, u32[]{:S(2)}, u32[]{:S(2)}) collective-permute-start(bf16[16,2,16]{2,0,1:T(8,128)(2,1)S(1)} %collective-permute-done.6), channel_id=1, source_target_pairs={{0,13},{1,0},{4,1},{5,4},{8,5},{9,8},{12,9},{13,12},{2,15},{3,2},{... | collective-permute-start | bytes 3080 | tf_op jit(solution)/shard_map/ppermute | solution.py:15
  71.6 4.9 %collective-permute-start.4 = (bf16[16,2,16]{2,0,1:T(8,128)(2,1)S(1)}, bf16[16,2,16]{2,0,1:T(8,128)(2,1)S(1)}, u32[]{:S(2)}, u32[]{:S(2)}) collective-permute-start(bf16[16,2,16]{2,0,1:T(8,128)(2,1)S(1)} %collective-permute-done.3), channel_id=1, source_target_pairs={{0,1},{1,4},{4,5},{5,8},{8,9},{9,12},{12,13},{13,0},{2,3},{3,6},{6... | collective-permute-start | bytes 3080 | tf_op jit(solution)/shard_map/ppermute | solution.py:13
  71.7 7.0 %collective-permute-start.8 = (bf16[16,2,16]{2,0,1:T(8,128)(2,1)S(1)}, bf16[16,2,16]{2,0,1:T(8,128)(2,1)S(1)}, u32[]{:S(2)}, u32[]{:S(2)}) collective-permute-start(bf16[16,2,16]{2,0,1:T(8,128)(2,1)S(1)} %collective-permute-done.7), channel_id=1, source_target_pairs={{0,13},{1,0},{4,1},{5,4},{8,5},{9,8},{12,9},{13,12},{2,15},{3,2},{... | collective-permute-start | bytes 3080 | tf_op jit(solution)/shard_map/ppermute | solution.py:15
  76.5 4.9 %collective-permute-start.5 = (bf16[16,2,16]{2,0,1:T(8,128)(2,1)S(1)}, bf16[16,2,16]{2,0,1:T(8,128)(2,1)S(1)}, u32[]{:S(2)}, u32[]{:S(2)}) collective-permute-start(bf16[16,2,16]{2,0,1:T(8,128)(2,1)S(1)} %collective-permute-done.4), channel_id=1, source_target_pairs={{0,1},{1,4},{4,5},{5,8},{8,9},{9,12},{12,13},{13,0},{2,3},{3,6},{6... | collective-permute-start | bytes 3080 | tf_op jit(solution)/shard_map/ppermute | solution.py:13
  78.7 4.2 %copy-start.3 = (bf16[16,2,64,128]{3,2,1,0:T(8,128)(2,1)S(1)}, bf16[16,2,64,128]{3,2,1,0:T(8,128)(2,1)}, u32[]{:S(2)}) copy-start(bf16[16,2,64,128]{3,2,1,0:T(8,128)(2,1)} %copy-done.2) | copy-start | bytes 1572868
  82.9 1.3 copy-start.8
  83.2 1.3 copy-start.7
  83.5 1.3 copy-start.6
  83.7 1.3 copy-start.5
  84.2 1.2 copy-start.4
  (3 other events, 2.5 us)
Sparse Core Ops, SparseCore 0:
  30.2 30.3 reduce-scatter.3
  86.5 68.3 all-reduce.2
